TPU v7x, 32 devices: a whole 2x2x4 slice. The times are simulated.
32 devices in a mesh: groups: 2 (over x), col: 16 (over z, y, core).
Axes of the slice: x: 2, y: 2, z: 4, core: 2. Of those that a mesh axis runs over, the one named last changes fastest.
Arguments:
- tokens: bfloat16 [4096, 4096], P(('groups', 'col')), parts along dimension 0, may hold values from -6 to 6
- weight_in: bfloat16 [4096, 1024], P('col'), may hold values from -0.09375 to 0.09375
- weight_out: bfloat16 [1024, 4096], P(None, 'col'), may hold values from -0.1875 to 0.1875
- up_quant: bfloat16 [16, 1024, 2688], P('col'), may hold values from -4 to 4
- up_scale: float32 [16, 8, 21], P('col'), may hold values from 0.0156 to 0.0625
- down_quant: bfloat16 [16, 2688, 1024], P('col'), may hold values from -4 to 4
- down_scale: float32 [16, 21, 8], P('col'), may hold values from 0.0097 to 0.0386
- routing: int32 [4096, 4], P(('groups', 'col')), parts along dimension 0, may hold values from 0 to 15, all different within a row; in each aligned block of 128 rows (0 to 127, 128 to 255, ...) at most 48 rows name the same one
- gate_weights: float32 [4096, 4], P(('groups', 'col')), parts along dimension 0, may hold values from 0.1 to 1
Outputs:
- mixed: bfloat16 [4096, 4096], P(('groups', 'col')), parts along dimension 0
There are 2 independent parts, one for each index of `groups`. A program takes and returns all parts, laid end to end along the dimension named above; an argument that names none is the same for every part. Nothing has to cross between parts.
Inputs may be any that keep to these rules, and one draw needn't show every extreme that they name: `routing`: each row names 4 different experts. Within the 128 rows of one index of col (aligned blocks) no expert is named more than 48 times, a bound that some block reaches.
All inputs are finite; a program needn't handle non-finite values.
Results may differ from a plain program's by a relative error of at most 0.0084.
Values may be sent and summed in bfloat16 or wider, within the bound.
A program may use at most 128 MiB of HBM per device.

v0:
```python
import jax
import jax.numpy as jnp
from jax import lax
from jax.sharding import PartitionSpec as P


def dequant(quant, scale):
    block = quant.shape[1] // scale.shape[1]
    expanded = jnp.repeat(jnp.repeat(scale, block, axis=-2), block, axis=-1)
    return (quant.astype(jnp.float32) * expanded).astype(jnp.bfloat16)


def body(
    tokens, weight_in, weight_out, up_quant, up_scale, down_quant, down_scale, routing, gate_weights
):
    tok_rows, top_count = routing.shape
    exp_local = up_quant.shape[0]
    n_devices = lax.axis_size("col")
    experts = exp_local * n_devices
    capacity = max(2, 3 * tok_rows * top_count // (2 * experts))
    width = weight_in.shape[1]
    slots_all = experts * capacity
    latent_sum = jnp.dot(
        tokens,
        lax.all_gather(weight_in, "col", axis=0, tiled=True),
        preferred_element_type=jnp.float32,
    )
    latent = latent_sum.astype(jnp.bfloat16)
    flat = routing.reshape(-1)
    onehot = (flat[:, None] == jnp.arange(experts, dtype=jnp.int32)[None, :]).astype(jnp.int32)
    before = jnp.cumsum(onehot, axis=0) - onehot
    slot_rank = jnp.sum(before * onehot, axis=1)
    target = flat * capacity + slot_rank
    hits = (target[:, None] == jnp.arange(slots_all, dtype=jnp.int32)[None, :]).astype(jnp.bfloat16)
    hits = jnp.sum(hits.reshape(tok_rows, top_count, slots_all), axis=1)
    outgoing = jnp.einsum("tr,tl->rl", hits, latent, preferred_element_type=jnp.float32).astype(
        jnp.bfloat16
    )
    outgoing = outgoing.reshape(n_devices, exp_local, capacity, width)
    up_w = dequant(up_quant, up_scale)
    down_w = dequant(down_quant, down_scale)
    piece = lax.all_to_all(outgoing, "col", split_axis=0, concat_axis=0, tiled=True)
    sources, local_count, count, lanes = piece.shape
    rows = piece.transpose(1, 0, 2, 3).reshape(local_count, sources * count, lanes)
    hidden = jnp.einsum("erl,elh->erh", rows, up_w, preferred_element_type=jnp.float32)
    act = jnp.square(jax.nn.relu(hidden)).astype(jnp.bfloat16)
    result = jnp.einsum("erh,ehl->erl", act, down_w, preferred_element_type=jnp.float32).astype(
        jnp.bfloat16
    )
    computed = result.reshape(local_count, sources, count, lanes).transpose(1, 0, 2, 3)
    returned = lax.all_to_all(computed, "col", split_axis=0, concat_axis=0, tiled=True)
    back_rows = returned.reshape(slots_all, width)
    picked = back_rows[target].reshape(tok_rows, top_count, width).astype(jnp.float32)
    combined = jnp.sum(picked * gate_weights[:, :, None], axis=1).astype(jnp.bfloat16)
    mixed = jnp.dot(
        combined,
        lax.all_gather(weight_out, "col", axis=1, tiled=True),
        preferred_element_type=jnp.float32,
    )
    return mixed.astype(jnp.bfloat16)


def solution(mesh):
    return jax.shard_map(
        body,
        mesh=mesh,
        in_specs=(
            P(("groups", "col"), None),
            P("col", None),
            P(None, "col"),
            P("col", None, None),
            P("col", None, None),
            P("col", None, None),
            P("col", None, None),
            P(("groups", "col"), None),
            P(("groups", "col"), None),
        ),
        out_specs=P(("groups", "col"), None),
        check_vma=False,
    )
```

profile of v0, /device:TPU:0, one launch (start us, length us, event | category | flops | bytes accessed | tf_op | source)
XLA Modules:
  0.0 231.6 jit_solution(3924298577807802875)
XLA Ops:
  6.5 0.7 all-gather.3.cloned.1.call-update
  7.3 0.7 all-gather.5.cloned.1.call-update
  8.0 0.8 copy.31
  8.9 0.1 eq.39
  9.0 1.2 reduce-window.6
  10.2 0.2 slice_reduce_fusion
  10.5 0.1 reduce_sum.35
  10.7 0.3 fusion.13
  11.0 76.1 %all-gather.3.cloned.1.call-done = bf16[4096,1024]{1,0:T(8,128)(2,1)} async-done(((bf16[256,1024]{1,0:T(8,128)(2,1)}), bf16[4096,1024]{1,0:T(8,128)(2,1)}) %all-gather.3.cloned.1.call-update) | async-done | bytes 8388624 | tf_op jit(solution)/shard_map/all_gather | solution.py:25
  87.2 6.2 %convolution_convert_fusion.1 = bf16[768,1024]{1,0:T(8,128)(2,1)} fusion(bf16[128,768]{1,0:T(8,128)(2,1)S(1)} %fusion.13, bf16[128,4096]{1,0:T(8,128)(2,1)S(1)} %copy-done, bf16[4096,1024]{1,0:T(8,128)(2,1)} %all-gather.3.cloned.1.call-done), kind=kOutput, calls=%fused_computation.10 | convolution fusion | flops 1275985920 | bytes 11206656 | tf_op jit(solution)/shard_map/tr,tl->rl/dot_general | solution.py:36
  93.4 3.9 %all-to-all-start = ((bf16[16,1,48,1024]{3,2,1,0:T(8,128)(2,1)}), bf16[16,1,48,1024]{3,2,1,0:T(8,128)(2,1)S(1)}, u32[]{:S(2)}, u32[]{:S(2)}) async-start(bf16[16,1,48,1024]{3,2,1,0:T(8,128)(2,1)} %bitcast.2), calls=%async_computation | async-start | bytes 3145728 | tf_op jit(solution)/shard_map/all_to_all | solution.py:42
  97.5 6.5 %broadcast_in_dim.31 = f32[2688,8,128]{2,1,0:T(8,128)} broadcast(f32[2688,8]{1,0:T(8,128)S(1)} %bitcast.61), dimensions={0,1} | broadcast | bytes 11096064 | tf_op jit(solution)/shard_map/broadcast_in_dim | solution.py:9
  104.0 12.6 %broadcast_in_dim.32 = f32[1,2688,1024]{2,1,0:T(8,128)} reshape(f32[2688,8,128]{2,1,0:T(8,128)} %broadcast_in_dim.31) | data formatting | bytes 22020096 | tf_op jit(solution)/shard_map/broadcast_in_dim | solution.py:9
  116.5 8.3 %copy.37 = bf16[1,1024,2688]{1,2,0:T(8,128)(2,1)} copy(bf16[1,1024,2688]{2,1,0:T(8,128)(2,1)} %param.12) | data formatting | bytes 11010048 | tf_op args[3]
  125.1 6.6 %fusion = bf16[1,1024,2688]{1,2,0:T(8,128)(2,1)} fusion(bf16[1,1024,2688]{1,2,0:T(8,128)(2,1)} %copy.37, f32[1024,21]{0,1:T(8,128)S(1)} %bitcast.64), kind=kLoop, calls=%fused_computation.2 | loop fusion | flops 8257536 | bytes 11096064 | tf_op jit(solution)/shard_map/convert_element_type | solution.py:10
  131.7 13.2 %all-to-all-done = bf16[16,1,48,1024]{3,2,1,0:T(8,128)(2,1)S(1)} async-done(((bf16[16,1,48,1024]{3,2,1,0:T(8,128)(2,1)}), bf16[16,1,48,1024]{3,2,1,0:T(8,128)(2,1)S(1)}, u32[]{:S(2)}, u32[]{:S(2)}) %all-to-all-start) | async-done | bytes 1572896 | tf_op jit(solution)/shard_map/all_to_all | solution.py:42
  144.9 18.6 %fusion.7 = bf16[768,1024]{1,0:T(8,128)(2,1)} fusion(f32[1,2688,1024]{2,1,0:T(8,128)} %broadcast_in_dim.32, bf16[1,2688,1024]{2,1,0:T(8,128)(2,1)} %param.14, bf16[768,1024]{1,0:T(8,128)(2,1)S(1)} %bitcast.62, bf16[1,1024,2688]{1,2,0:T(8,128)(2,1)} %fusion), kind=kOutput, calls=%fused_computation.11 | convolution fusion | flops 8470953984 | bytes 25165824 | tf_op jit(solution)/shard_map/erh,ehl->erl/dot_general | solution.py:47
  163.4 8.2 %all-to-all-start.1 = ((bf16[16,1,48,1024]{3,2,1,0:T(8,128)(2,1)}), bf16[16,1,48,1024]{3,2,1,0:T(8,128)(2,1)S(1)}, u32[]{:S(2)}, u32[]{:S(2)}) async-start(bf16[16,1,48,1024]{3,2,1,0:T(8,128)(2,1)} %bitcast.63), calls=%async_computation.1 | async-start | bytes 3145728 | tf_op jit(solution)/shard_map/all_to_all | solution.py:51
  171.8 0.1 copy.41
  171.9 43.0 %all-to-all-done.1 = bf16[16,1,48,1024]{3,2,1,0:T(8,128)(2,1)S(1)} async-done(((bf16[16,1,48,1024]{3,2,1,0:T(8,128)(2,1)}), bf16[16,1,48,1024]{3,2,1,0:T(8,128)(2,1)S(1)}, u32[]{:S(2)}, u32[]{:S(2)}) %all-to-all-start.1) | async-done | bytes 1572896 | tf_op jit(solution)/shard_map/all_to_all | solution.py:51
  214.9 2.0 gather_fusion
  217.0 0.7 reshape.113
  217.7 1.4 multiply_reduce_fusion
  219.1 5.6 %convolution_convert_fusion = bf16[128,4096]{1,0:T(8,128)(2,1)} fusion(bf16[1024,4096]{1,0:T(8,128)(2,1)} %all-gather.5.cloned.1.call-done, bf16[128,1024]{1,0:T(8,128)(2,1)S(1)} %multiply_reduce_fusion), kind=kOutput, calls=%fused_computation.8 | convolution fusion | flops 1074266112 | bytes 9699328 | tf_op jit(solution)/shard_map/dot_general | solution.py:55
  (29 shorter events, 0.9 us)
Async XLA Ops:
  6.5 80.6 %copy-start = (bf16[128,4096]{1,0:T(8,128)(2,1)S(1)}, bf16[128,4096]{1,0:T(8,128)(2,1)}, u32[]{:S(2)}) copy-start(bf16[128,4096]{1,0:T(8,128)(2,1)} %param.9) | copy-start | bytes 3145732
  6.5 80.6 %all-gather.3.cloned.1.call-start = ((), (), s32[]{:S(2)}) async-start(), calls=%async_computation.2 | async-start | bytes 8912896 | tf_op jit(solution)/shard_map/all_gather | solution.py:25
  7.3 211.8 %all-gather.5.cloned.1.call-start = ((), (), s32[]{:S(2)}) async-start(), calls=%async_computation.3 | async-start | bytes 8912896 | tf_op jit(solution)/shard_map/all_gather | solution.py:57
  11.0 86.3 %copy-start.2 = (f32[1,21,8]{1,2,0:T(8,128)S(1)}, f32[1,21,8]{1,2,0:T(8,128)}, u32[]{:S(2)}) copy-start(f32[1,21,8]{1,2,0:T(8,128)} %param.15) | copy-start | bytes 2020
  93.4 51.5 %all-to-all-start = ((bf16[16,1,48,1024]{3,2,1,0:T(8,128)(2,1)}), bf16[16,1,48,1024]{3,2,1,0:T(8,128)(2,1)S(1)}, u32[]{:S(2)}, u32[]{:S(2)}) async-start(bf16[16,1,48,1024]{3,2,1,0:T(8,128)(2,1)} %bitcast.2), calls=%async_computation | async-start | bytes 3145728 | tf_op jit(solution)/shard_map/all_to_all | solution.py:42
  116.5 8.3 %copy-start.3 = (f32[1,8,21]{2,1,0:T(8,128)S(1)}, f32[1,8,21]{2,1,0:T(8,128)}, u32[]{:S(2)}) copy-start(f32[1,8,21]{2,1,0:T(8,128)} %param.13) | copy-start | bytes 2020
  144.9 26.9 %copy-start.4 = (f32[128,4]{0,1:T(4,128)S(1)}, f32[128,4]{0,1:T(4,128)}, u32[]{:S(2)}) copy-start(f32[128,4]{0,1:T(4,128)} %param.17) | copy-start | bytes 6148
  163.4 51.5 %all-to-all-start.1 = ((bf16[16,1,48,1024]{3,2,1,0:T(8,128)(2,1)}), bf16[16,1,48,1024]{3,2,1,0:T(8,128)(2,1)S(1)}, u32[]{:S(2)}, u32[]{:S(2)}) async-start(bf16[16,1,48,1024]{3,2,1,0:T(8,128)(2,1)} %bitcast.63), calls=%async_computation.1 | async-start | bytes 3145728 | tf_op jit(solution)/shard_map/all_to_all | solution.py:51
  217.7 7.0 %copy-start.1 = (bf16[128,4096]{1,0:T(8,128)(2,1)S(1)}, bf16[128,4096]{1,0:T(8,128)(2,1)}, u32[]{:S(2)}) copy-start(bf16[128,4096]{1,0:T(8,128)(2,1)} %param.9) | copy-start | bytes 3145732
Sparse Core Ops, SparseCore 0:
  9.5 77.5 all-gather.2
  89.3 123.9 all-gather.4
where the time goes:
time: 236 us; the launch traced here: 232 us
  waiting for transfers between devices  134 us (57%)
  local copies, waits for them, and re-layouts  32.2 us (14%)
  matrix products  30.4 us (13%)
  between operations  13.6 us (6%)
  starting transfers between devices  12.2 us (5%)
  other arithmetic  9.52 us (4%)
    all_gather x1, waiting for transfers between devices, body(): lax.all_gather(weight_in, 'col', axis=0, tiled=True)  76.1 us
    all_to_all x1, waiting for transfers between devices, body(): lax.all_to_all(computed, 'col', split_axis=0, concat_axis=0, tiled=True)  43 us
    broadcast_in_dim x3, local copies, waits for them, and re-layouts, dequant(): expanded = jnp.repeat(jnp.repeat(scale, block, axis=-2), block, axis=-1)  19.2 us
    dot_general x1, matrix products, body(): jnp.einsum('erh,ehl->erl', act, down_w, preferred_element_type=jnp.float32)  18.6 us
    all_to_all x1, waiting for transfers between devices, body(): lax.all_to_all(outgoing, 'col', split_axis=0, concat_axis=0, tiled=True)  13.2 us
    unnamed x16, local copies, waits for them, and re-layouts  9.35 us
    all_to_all x1, starting transfers between devices, body(): lax.all_to_all(computed, 'col', split_axis=0, concat_axis=0, tiled=True)  8.23 us
    convert_element_type x1, other arithmetic, dequant(): return (quant.astype(jnp.float32) * expanded).astype(jnp.bfloat16)  6.57 us
  transfers between devices with their start and end apart: 4, of which 3 were waited for; matrix products, arithmetic and copies ran while one was open for 29% of the time, Pallas kernels for 0%

commit v1 on v0

v1 whole, which is shorter than its diff:
```python
import functools

import jax
import jax.numpy as jnp
from jax import lax
from jax.experimental import pallas as pl
from jax.experimental.pallas import tpu as pltpu
from jax.sharding import PartitionSpec as P

QUAD = 4
CHUNK = 4
MESH = pl.DeviceIdType.MESH
F32, BF16 = jnp.float32, jnp.bfloat16


def dequant(quant, scale):
    block = quant.shape[1] // scale.shape[1]
    expanded = jnp.repeat(jnp.repeat(scale, block, axis=-2), block, axis=-1)
    return (quant.astype(F32) * expanded).astype(BF16)


def capacity_of(tok_rows, top_count, experts):
    return max(2, 3 * tok_rows * top_count // (2 * experts))


def plain_body(
    tokens, weight_in, weight_out, up_quant, up_scale, down_quant, down_scale, routing, gate_weights
):
    tok_rows, top_count = routing.shape
    exp_local = up_quant.shape[0]
    n_devices = lax.axis_size("col")
    experts = exp_local * n_devices
    capacity = capacity_of(tok_rows, top_count, experts)
    width = weight_in.shape[1]
    slots_all = experts * capacity
    latent = jnp.dot(
        tokens,
        lax.all_gather(weight_in, "col", axis=0, tiled=True),
        preferred_element_type=F32,
    ).astype(BF16)
    flat = routing.reshape(-1)
    onehot = (flat[:, None] == jnp.arange(experts, dtype=jnp.int32)[None, :]).astype(BF16)
    places = jnp.arange(flat.shape[0], dtype=jnp.int32)
    earlier = (places[:, None] > places[None, :]).astype(BF16)
    before = jnp.dot(earlier, onehot, preferred_element_type=F32)
    slot_rank = jnp.sum(before * onehot.astype(F32), axis=1).astype(jnp.int32)
    target = flat * capacity + slot_rank
    hits = (target[:, None] == jnp.arange(slots_all, dtype=jnp.int32)[None, :]).astype(BF16)
    hits = jnp.sum(hits.reshape(tok_rows, top_count, slots_all), axis=1)
    outgoing = jnp.einsum("tr,tl->rl", hits, latent, preferred_element_type=F32).astype(BF16)
    outgoing = outgoing.reshape(n_devices, exp_local, capacity, width)
    up_w = dequant(up_quant, up_scale)
    down_w = dequant(down_quant, down_scale)
    piece = lax.all_to_all(outgoing, "col", split_axis=0, concat_axis=0, tiled=True)
    sources, local_count, count, lanes = piece.shape
    rows = piece.transpose(1, 0, 2, 3).reshape(local_count, sources * count, lanes)
    hidden = jnp.einsum("erl,elh->erh", rows, up_w, preferred_element_type=F32)
    act = jnp.square(jax.nn.relu(hidden)).astype(BF16)
    result = jnp.einsum("erh,ehl->erl", act, down_w, preferred_element_type=F32).astype(BF16)
    computed = result.reshape(local_count, sources, count, lanes).transpose(1, 0, 2, 3)
    returned = lax.all_to_all(computed, "col", split_axis=0, concat_axis=0, tiled=True)
    back_rows = returned.reshape(slots_all, width)
    picked = back_rows[target].reshape(tok_rows, top_count, width).astype(F32)
    combined = jnp.sum(picked * gate_weights[:, :, None], axis=1).astype(BF16)
    mixed = jnp.dot(
        combined,
        lax.all_gather(weight_out, "col", axis=1, tiled=True),
        preferred_element_type=F32,
    )
    return mixed.astype(BF16)


def layer_kernel(
    n, n_groups, cap,
    tokens, w_in, w_out, upq, ups, dnq, dns, routing, gates,
    out,
    win, tq, tr, ps, pr, lat, hits, ghi, glo, disp, rows_in, res, back, upw, dnw, act, wl, comb, cr,
    sb, out_v,
    s_local, s_tq, s_win, r_win, s_winx, r_winx, s_tok, r_tok, s_par, r_par, s_disp, r_disp, s_ret, r_ret,
    s_wo, r_wo, s_woy, r_woy, s_wox, r_wox, s_comb, r_comb, s_out, r_out,
):
    lines = n // QUAD
    half = QUAD // 2
    toks = tokens.shape[0]
    kd, wide = w_in.shape
    wd = w_out.shape[1]
    hid = upw.shape[1]
    top = routing.shape[1]
    slots = n * cap
    me, grp = lax.axis_index("col"), lax.axis_index("groups")
    z, q = me // QUAD, lax.rem(me, QUAD)

    def at(col):
        return (grp, col)

    def across(step):
        return (lax.rem(grp + step, n_groups), me)

    def remote(src, dst, send, recv, to):
        return pltpu.make_async_remote_copy(
            src_ref=src, dst_ref=dst, send_sem=send, recv_sem=recv, device_id=to, device_id_type=MESH
        )

    tok_loads = []
    for i in range(n):
        line, lane = i // QUAD, i % QUAD
        tok_loads.append(
            pltpu.make_async_copy(
                tokens.at[:, pl.ds(i * kd, kd)], tq.at[lane, :, pl.ds(line * kd, kd)], s_tq.at[i]
            )
        )
    my_rows = pl.ds(pl.multiple_of(z * kd, kd), kd)
    loads = [
        pltpu.make_async_copy(w_in, win.at[my_rows], s_local.at[0]),
        pltpu.make_async_copy(upq, upw, s_local.at[1]),
        pltpu.make_async_copy(dnq, dnw, s_local.at[2]),
        pltpu.make_async_copy(w_out, wl.at[0, z], s_local.at[3]),
    ]
    for c in tok_loads:
        c.start()
    for c in loads:
        c.start()

    barrier = pltpu.get_barrier_semaphore()
    for d in range(1, n):
        pl.semaphore_signal(barrier, inc=1, device_id=at(lax.rem(me + d, n)), device_id_type=MESH)
    for d in range(1, n_groups):
        pl.semaphore_signal(barrier, inc=1, device_id=across(d), device_id_type=MESH)
    pl.semaphore_wait(barrier, n - 1 + n_groups - 1)

    kp = kd // n_groups
    win_sends = []
    for d in range(1, lines):
        src = w_in.at[pl.ds(pl.multiple_of(grp * kp, kp), kp)]
        dst = win.at[pl.ds(pl.multiple_of(z * kd + grp * kp, kp), kp)]
        c = remote(src, dst, s_win.at[d - 1], r_win.at[d - 1], at(lax.rem(z + d, lines) * QUAD + q))
        c.start()
        win_sends.append(c)
    for c in tok_loads:
        c.wait()
    tok_sends = []
    for d in range(1, QUAD):
        to = lax.rem(q + d, QUAD)
        c = remote(tq.at[to], tr.at[d - 1], s_tok.at[d - 1], r_tok.at[d - 1], at(z * QUAD + to))
        c.start()
        tok_sends.append(c)

    lane_e = lax.broadcasted_iota(jnp.int32, (toks, n), 1)
    mask = jnp.zeros((toks, n), F32)
    gate = jnp.zeros((toks, n), F32)
    for k in range(top):
        eq = (routing[:, k : k + 1] == lane_e).astype(F32)
        mask = mask + eq
        gate = gate + eq * gates[:, k : k + 1]
    earlier = (
        lax.broadcasted_iota(jnp.int32, (toks, toks), 0) > lax.broadcasted_iota(jnp.int32, (toks, toks), 1)
    ).astype(F32).astype(BF16)
    rank = jnp.dot(earlier, mask.astype(BF16), preferred_element_type=F32)
    out_of_range = -float(1 << slots.bit_length())
    rank = jnp.where(mask > 0.5, rank, out_of_range).astype(BF16)
    row = lax.broadcasted_iota(jnp.int32, (n, slots), 0)
    col = lax.broadcasted_iota(jnp.int32, (n, slots), 1)
    inside = ((col >= row * cap) & (col < row * cap + cap)).astype(F32)
    start = jnp.sum(inside * (row * cap).astype(F32), axis=0, keepdims=True)
    spread = inside.astype(BF16)
    rank_x = jnp.dot(rank, spread, preferred_element_type=F32)
    slot = lax.broadcasted_iota(jnp.int32, (toks, slots), 1).astype(F32)
    hit = (rank_x + start == slot).astype(F32)
    hits[...] = hit.astype(BF16)
    gate_hi = gate.astype(BF16)
    gate_lo = (gate - gate_hi.astype(F32)).astype(BF16)
    ghi[...] = (hit * jnp.dot(gate_hi, spread, preferred_element_type=F32)).astype(BF16)
    glo[...] = (hit * jnp.dot(gate_lo, spread, preferred_element_type=F32)).astype(BF16)

    def expand(weights, scales):
        rows_n, cols_n = scales.shape
        br, bc = weights.shape[0] // rows_n, weights.shape[1] // cols_n

        def step(i, carry):
            rows = pl.ds(pl.multiple_of(i * br, br), br)
            for j in range(cols_n):
                cols = slice(j * bc, (j + 1) * bc)
                weights[rows, cols] = (weights[rows, cols].astype(F32) * scales[i, j]).astype(BF16)
            return carry

        lax.fori_loop(0, rows_n, step, 0)

    loads[1].wait()
    expand(upw, ups)

    winx_sends = []
    for d in range(1, lines):
        win_sends[d - 1].wait_recv()
        src = win.at[pl.ds(pl.multiple_of(lax.rem(z + lines - d, lines) * kd + grp * kp, kp), kp)]
        for e in range(1, n_groups):
            i = (d - 1) * (n_groups - 1) + e - 1
            c = remote(src, src, s_winx.at[i], r_winx.at[i], across(e))
            c.start()
            winx_sends.append(c)

    op = wide // n_groups
    mine = pl.ds(pl.multiple_of(grp * op, op), op)
    wo_sends = []
    for d in range(1, lines):
        c = remote(
            w_out.at[mine], wl.at[0, z, mine], s_wo.at[d - 1], r_wo.at[d - 1],
            at(lax.rem(z + d, lines) * QUAD + q),
        )
        c.start()
        wo_sends.append(c)
    y_peer = at(z * QUAD + lax.rem(q + half, QUAD))
    woy_sends = [remote(w_out.at[mine], wl.at[1, z, mine], s_woy.at[0], r_woy.at[0], y_peer)]

    loads[2].wait()
    expand(dnw, dns)

    loads[0].wait()
    for c in winx_sends:
        c.wait_recv()
    for c in tok_sends:
        c.wait_recv()

    part = jnp.dot(
        tr[...].reshape((QUAD - 1) * toks, lines * kd), win[...], preferred_element_type=F32
    ).astype(BF16)
    ps[...] = part.reshape(QUAD - 1, toks, wide)
    par_sends = []
    for d in range(1, QUAD):
        c = remote(
            ps.at[d - 1], pr.at[d - 1], s_par.at[d - 1], r_par.at[d - 1],
            at(z * QUAD + lax.rem(q + QUAD - d, QUAD)),
        )
        c.start()
        par_sends.append(c)
    total = jnp.dot(tq[q], win[...], preferred_element_type=F32)
    for d in range(1, QUAD):
        par_sends[d - 1].wait_recv()
        total = total + pr[d - 1].astype(F32)
    lat[...] = total.astype(BF16)

    disp[...] = lax.dot_general(
        hits[...], lat[...], (((0,), (0,)), ((), ())), preferred_element_type=F32
    ).astype(BF16)

    def block(i):
        return pl.ds(pl.multiple_of(i * cap, cap), cap)

    def dispatch(d):
        to = lax.rem(me + d, n)
        return remote(disp.at[block(to)], rows_in.at[block(d)], s_disp.at[d], r_disp.at[d], at(to))

    def give_back(d):
        to = lax.rem(me + n - d, n)
        return remote(res.at[block(d)], back.at[block(me)], s_ret.at[d], r_ret.at[d], at(to))

    for d in range(1, n):
        dispatch(d).start()
    rows_in[0:cap] = disp[block(me)]

    woy_sends[0].start()
    wox_sends = []

    def over_groups(ref):
        for e in range(1, n_groups):
            i = len(wox_sends)
            c = remote(ref, ref, s_wox.at[i], r_wox.at[i], across(e))
            c.start()
            wox_sends.append(c)

    for d in range(1, lines):
        wo_sends[d - 1].wait_recv()
        frm = lax.rem(z + lines - d, lines)
        c = remote(wl.at[0, frm, mine], wl.at[1, frm, mine], s_woy.at[d], r_woy.at[d], y_peer)
        c.start()
        woy_sends.append(c)
        over_groups(wl.at[0, frm, mine])

    def chunk(k, carry):
        for i in range(CHUNK):
            d = k * CHUNK + i

            @pl.when(d > 0)
            def _():
                dispatch(d).wait_recv()

        rows = pl.ds(pl.multiple_of(k * CHUNK * cap, CHUNK * cap), CHUNK * cap)
        hidden = jnp.dot(rows_in[rows], upw[...], preferred_element_type=F32)
        act[...] = jnp.square(jnp.maximum(hidden, 0.0)).astype(BF16)
        res[rows] = jnp.dot(act[...], dnw[...], preferred_element_type=F32).astype(BF16)
        for i in range(CHUNK):
            d = k * CHUNK + i

            @pl.when(d > 0)
            def _():
                give_back(d).start()

        return carry

    lax.fori_loop(0, n // CHUNK, chunk, 0)

    for d in range(lines):
        woy_sends[d].wait_recv()
        over_groups(wl.at[1, lax.rem(z + lines - d, lines), mine])

    back[block(me)] = res[0:cap]
    for d in range(1, n):
        give_back(d).wait_recv()
    combined = jnp.dot(ghi[...], back[...], preferred_element_type=F32) + jnp.dot(
        glo[...], back[...], preferred_element_type=F32
    )
    comb[0:toks] = combined.astype(BF16)
    pair = at(z * QUAD + q + 1 - 2 * lax.rem(q, 2))
    share = remote(comb.at[0:toks], comb.at[toks : 2 * toks], s_comb, r_comb, pair)
    share.start()
    loads[3].wait()
    for c in wox_sends:
        c.wait_recv()
    share.wait_recv()

    def columns(i):
        owner = lax.rem(i, lines) * QUAD + lax.rem(q + half * (i // lines), QUAD)
        return pl.ds(pl.multiple_of(owner * wd, wd), wd)

    def hand_over(i):
        return remote(sb.at[i], out_v.at[:, columns(i)], s_out.at[i], r_out.at[i], pair)

    def project(i, carry):
        both = jnp.dot(
            comb[...], wl[i // lines, lax.rem(i, lines)], preferred_element_type=F32
        ).astype(BF16)
        out_v[:, columns(i)] = both[0:toks]
        sb[i] = both[toks : 2 * toks]
        hand_over(i).start()
        return carry

    lax.fori_loop(0, 2 * lines, project, 0)
    for i in range(2 * lines):
        hand_over(i).wait_recv()
    final = pltpu.make_async_copy(out_v, out, s_local.at[4])
    final.start()
    for c in win_sends + winx_sends + tok_sends + par_sends + wo_sends + woy_sends + wox_sends + [share]:
        c.wait_send()
    for d in range(1, n):
        dispatch(d).wait_send()
        give_back(d).wait_send()
    for i in range(2 * lines):
        hand_over(i).wait_send()
    final.wait()


def kernel_body(
    n, n_groups,
    tokens, weight_in, weight_out, up_quant, up_scale, down_quant, down_scale, routing, gate_weights,
):
    toks, top = routing.shape
    cap = -(-capacity_of(toks, top, n) // 16) * 16
    lines = n // QUAD
    kd, wide = weight_in.shape
    wd = weight_out.shape[1]
    hid = up_quant.shape[2]
    slots = n * cap

    def vm(*shape):
        return pltpu.VMEM(shape, BF16)

    def sem(*shape):
        return pltpu.SemaphoreType.DMA(shape)

    others = n_groups - 1
    hbm = pl.BlockSpec(memory_space=pl.ANY)
    smem = pl.BlockSpec(memory_space=pltpu.SMEM)
    vmem = pl.BlockSpec(memory_space=pltpu.VMEM)
    flops = 2 * toks * kd * n * wide + 4 * slots * wide * hid + 2 * toks * wide * wd * n
    return pl.pallas_call(
        functools.partial(layer_kernel, n, n_groups, cap),
        out_shape=jax.ShapeDtypeStruct((toks, wd * n), BF16),
        in_specs=[hbm, hbm, hbm, hbm, smem, hbm, smem, vmem, vmem],
        out_specs=hbm,
        scratch_shapes=[
            vm(lines * kd, wide),
            vm(QUAD, toks, lines * kd),
            vm(QUAD - 1, toks, lines * kd),
            vm(QUAD - 1, toks, wide),
            vm(QUAD - 1, toks, wide),
            vm(toks, wide),
            vm(toks, slots),
            vm(toks, slots),
            vm(toks, slots),
            vm(slots, wide),
            vm(slots, wide),
            vm(slots, wide),
            vm(slots, wide),
            vm(wide, hid),
            vm(hid, wide),
            vm(CHUNK * cap, hid),
            vm(2, lines, wide, wd),
            vm(2 * toks, wide),
            vm(16, 128),
            vm(2 * lines, toks, wd),
            vm(toks, wd * n),
            sem(5), sem(n),
            sem(lines), sem(lines), sem(lines * others + 1), sem(lines * others + 1),
            sem(QUAD), sem(QUAD), sem(QUAD), sem(QUAD),
            sem(n), sem(n), sem(n), sem(n),
            sem(lines), sem(lines), sem(lines), sem(lines),
            sem(2 * lines * others + 1), sem(2 * lines * others + 1),
            pltpu.SemaphoreType.DMA, pltpu.SemaphoreType.DMA,
            sem(2 * lines), sem(2 * lines),
        ],
        compiler_params=pltpu.CompilerParams(
            collective_id=0, has_side_effects=True, vmem_limit_bytes=52 * 2**20
        ),
        cost_estimate=pl.CostEstimate(flops=flops, bytes_accessed=32 * 2**20, transcendentals=0),
    )(
        tokens, weight_in, weight_out,
        up_quant.reshape(wide, hid), up_scale.reshape(up_scale.shape[1:]),
        down_quant.reshape(hid, wide), down_scale.reshape(down_scale.shape[1:]),
        routing, gate_weights,
    )


def solution(mesh):
    n, n_groups = mesh.shape["col"], mesh.shape["groups"]

    def body(*args):
        tokens, weight_in, weight_out, up_quant = args[:4]
        fits = (
            n % QUAD == 0
            and (n // CHUNK) * CHUNK == n
            and up_quant.shape[0] == 1
            and weight_in.shape[0] % 128 == 0
            and weight_out.shape[1] % 128 == 0
        )
        if fits:
            return kernel_body(n, n_groups, *args)
        return plain_body(*args)

    return jax.shard_map(
        body,
        mesh=mesh,
        in_specs=(
            P(("groups", "col"), None),
            P("col", None),
            P(None, "col"),
            P("col", None, None),
            P("col", None, None),
            P("col", None, None),
            P("col", None, None),
            P(("groups", "col"), None),
            P(("groups", "col"), None),
        ),
        out_specs=P(("groups", "col"), None),
        check_vma=False,
    )
```

time: 236 us -> 151 us (0.64); the launches traced: 232 us -> 151 us
  Pallas kernels: 0 us -> 144 us
  waiting for transfers between devices: 134 us -> 0 us
  matrix products: 30.4 us -> 0 us
  local copies, waits for them, and re-layouts: 32.2 us -> 7.4 us
  between operations: 13.6 us -> 0.02 us
  starting transfers between devices: 12.2 us -> 0 us
  other arithmetic: 9.52 us -> 0 us
    pallas_call x0 -> x1, Pallas kernels: none -> 144 us  [kernel_body(): pl.pallas_call(functools.partial(layer_kernel, n, n_groups, cap), out_sha...]
    all_gather x2 -> x0, waiting for transfers between devices: 76.2 us -> none  [the longest x1 76.1 us: body(): lax.all_gather(weight_in, 'col', axis=0, tiled=True)]
    all_to_all x2 -> x0, waiting for transfers between devices: 56.2 us -> none  [the longest x1 43 us: body(): lax.all_to_all(computed, 'col', split_axis=0, concat_axis=0, tiled=True)]
    dot_general x3 -> x0, matrix products: 30.4 us -> none  [the longest x1 18.6 us: body(): jnp.einsum('erh,ehl->erl', act, down_w, preferred_element_type=jnp.float32)]
    broadcast_in_dim x3 -> x0, local copies, waits for them, and re-layouts: 19.2 us -> none  [dequant(): expanded = jnp.repeat(jnp.repeat(scale, block, axis=-2), block, axis=-1)]
    all_to_all x2 -> x0, starting transfers between devices: 12.1 us -> none  [the longest x1 8.23 us: body(): lax.all_to_all(computed, 'col', split_axis=0, concat_axis=0, tiled=True)]
    convert_element_type x2 -> x0, other arithmetic: 6.57 us -> none  [the longest x1 6.57 us: dequant(): return (quant.astype(jnp.float32) * expanded).astype(jnp.bfloat16)]
    unnamed x16 -> x10, local copies, waits for them, and re-layouts: 9.35 us -> 7.4 us
  transfers between devices with their start and end apart: 4 -> 0, of which waited for: 3 -> 0; matrix products, arithmetic and copies ran while one was open for 29% -> 0% of each run, Pallas kernels for 0% -> 0%
where the time goes in v1:
time: 151 us
  Pallas kernels  144 us (95%)
  local copies, waits for them, and re-layouts  7.4 us (5%)
    pallas_call x1, Pallas kernels, kernel_body(): pl.pallas_call(functools.partial(layer_kernel, n, n_groups, cap), out_sha...  144 us
    unnamed x10, local copies, waits for them, and re-layouts  7.4 us

profile of v1, /device:TPU:0, one launch (start us, length us, event | category | flops | bytes accessed | tf_op | source)
XLA Modules:
  0.0 151.1 jit_solution(11379281553822428547)
XLA Ops:
  0.0 0.8 copy.10
  0.8 0.8 copy.11.routing
  1.6 0.8 copy.12.gates
  2.3 0.0 copy-start
  2.4 1.0 copy-done
  3.4 0.0 copy-start.1
  3.4 1.0 copy-done.1
  4.4 0.0 copy-start.2
  4.4 0.7 copy-done.2
  5.1 143.7 %shard_map.91 = bf16[128,4096]{1,0:T(8,128)(2,1)} custom-call(bf16[128,4096]{1,0:T(8,128)(2,1)} %tokens.1, bf16[256,1024]{1,0:T(8,128)(2,1)S(1)} %copy-done, bf16[1024,256]{1,0:T(8,128)(2,1)S(1)} %copy-done.1, bf16[1024,2688]{1,0:T(8,128)(2,1)} %bitcast.6, f32[8,21]{1,0:T(8,128)S(1)} %bitcast.5, bf16[2688,1024]{1,0:T(8,128)(2,1)} %bitcast.7, ...), custom_call_target="tpu_custom_call" | custom-call | flops 10603200512 | bytes 33554432 | tf_op jit(solution)/shard_map/pallas_call | solution.py:374
  148.9 2.3 %copy.14 = bf16[128,4096]{1,0:T(8,128)(2,1)} copy(bf16[128,4096]{1,0:T(8,128)(2,1)} %shard_map.91) | data formatting | bytes 2097152
Async XLA Ops:
  2.3 1.0 copy-start
  3.4 1.0 copy-start.1
  4.4 0.7 copy-start.2

commit v2 on v1

--- a/solution.py
+++ b/solution.py
@@ -8,7 +8,6 @@
 from jax.sharding import PartitionSpec as P
 
 QUAD = 4
-CHUNK = 4
 MESH = pl.DeviceIdType.MESH
 F32, BF16 = jnp.float32, jnp.bfloat16
 
@@ -74,9 +73,9 @@
     n, n_groups, cap,
     tokens, w_in, w_out, upq, ups, dnq, dns, routing, gates,
     out,
-    win, tq, tr, ps, pr, lat, hits, ghi, glo, disp, rows_in, res, back, upw, dnw, act, wl, comb, cr,
+    win, tq, tr, ps, pr, plan, lat, hits, ghi, glo, disp, rows_in, res, back, mine_part, parts, upw, dnw, act, wl, comb,
     sb, out_v,
-    s_local, s_tq, s_win, r_win, s_winx, r_winx, s_tok, r_tok, s_par, r_par, s_disp, r_disp, s_ret, r_ret,
+    s_local, s_tq, s_win, r_win, s_winx, r_winx, s_tok, r_tok, s_par, r_par, s_plan, r_plan, s_lat, r_lat, s_sum, r_sum, s_disp, r_disp, s_ret, r_ret,
     s_wo, r_wo, s_woy, r_woy, s_wox, r_wox, s_comb, r_comb, s_out, r_out,
 ):
     lines = n // QUAD
@@ -129,13 +128,26 @@
     pl.semaphore_wait(barrier, n - 1 + n_groups - 1)
 
     kp = kd // n_groups
-    win_sends = []
-    for d in range(1, lines):
-        src = w_in.at[pl.ds(pl.multiple_of(grp * kp, kp), kp)]
-        dst = win.at[pl.ds(pl.multiple_of(z * kd + grp * kp, kp), kp)]
-        c = remote(src, dst, s_win.at[d - 1], r_win.at[d - 1], at(lax.rem(z + d, lines) * QUAD + q))
-        c.start()
-        win_sends.append(c)
+    def win_piece(owner):
+        return win.at[pl.ds(pl.multiple_of(owner * kd + grp * kp, kp), kp)]
+
+    def hop(way, j):
+        owner = jnp.clip(z - way * j, 0, lines - 1)
+        nxt = jnp.clip(z + way, 0, lines - 1)
+        i = j if way > 0 else lines + j
+        return remote(win_piece(owner), win_piece(owner), s_win.at[i], r_win.at[i], at(nxt * QUAD + q))
+
+    def hop_over(way, j, e):
+        owner = jnp.clip(z - way * (j + 1), 0, lines - 1)
+        i = ((j if way > 0 else lines + j) * n_groups) + e
+        return remote(win_piece(owner), win_piece(owner), s_winx.at[i], r_winx.at[i], across(e))
+
+    def has(way, j):
+        return (z - way * j >= 0) & (z - way * j < lines)
+
+    loads[0].wait()
+    for way in (1, -1):
+        pl.when(has(way, -1))(hop(way, 0).start)
     for c in tok_loads:
         c.wait()
     tok_sends = []
@@ -158,19 +170,27 @@
     rank = jnp.dot(earlier, mask.astype(BF16), preferred_element_type=F32)
     out_of_range = -float(1 << slots.bit_length())
     rank = jnp.where(mask > 0.5, rank, out_of_range).astype(BF16)
-    row = lax.broadcasted_iota(jnp.int32, (n, slots), 0)
-    col = lax.broadcasted_iota(jnp.int32, (n, slots), 1)
-    inside = ((col >= row * cap) & (col < row * cap + cap)).astype(F32)
-    start = jnp.sum(inside * (row * cap).astype(F32), axis=0, keepdims=True)
-    spread = inside.astype(BF16)
-    rank_x = jnp.dot(rank, spread, preferred_element_type=F32)
-    slot = lax.broadcasted_iota(jnp.int32, (toks, slots), 1).astype(F32)
-    hit = (rank_x + start == slot).astype(F32)
-    hits[...] = hit.astype(BF16)
     gate_hi = gate.astype(BF16)
     gate_lo = (gate - gate_hi.astype(F32)).astype(BF16)
-    ghi[...] = (hit * jnp.dot(gate_hi, spread, preferred_element_type=F32)).astype(BF16)
-    glo[...] = (hit * jnp.dot(gate_lo, spread, preferred_element_type=F32)).astype(BF16)
+    lanes = plan.shape[2]
+
+    def placed(part, values):
+        shift = (
+            lax.broadcasted_iota(jnp.int32, (n, lanes), 0) + part * n
+            == lax.broadcasted_iota(jnp.int32, (n, lanes), 1)
+        )
+        return jnp.dot(values, shift.astype(F32).astype(BF16), preferred_element_type=F32)
+
+    plan[0] = (placed(0, rank) + placed(1, gate_hi) + placed(2, gate_lo)).astype(BF16)
+
+    def along(s, src, dst, send, recv):
+        return remote(src, dst, send, recv, at(lax.rem(z + s, lines) * QUAD + q))
+
+    plan_sends = []
+    for s in range(1, lines):
+        c = along(s, plan.at[0], plan.at[s], s_plan.at[s], r_plan.at[s])
+        c.start()
+        plan_sends.append(c)
 
     def expand(weights, scales):
         rows_n, cols_n = scales.shape
@@ -185,18 +205,15 @@
 
         lax.fori_loop(0, rows_n, step, 0)
 
-    loads[1].wait()
-    expand(upw, ups)
-
-    winx_sends = []
-    for d in range(1, lines):
-        win_sends[d - 1].wait_recv()
-        src = win.at[pl.ds(pl.multiple_of(lax.rem(z + lines - d, lines) * kd + grp * kp, kp), kp)]
-        for e in range(1, n_groups):
-            i = (d - 1) * (n_groups - 1) + e - 1
-            c = remote(src, src, s_winx.at[i], r_winx.at[i], across(e))
-            c.start()
-            winx_sends.append(c)
+    for j in range(lines - 1):
+        for way in (1, -1):
+            @pl.when(has(way, j + 1))
+            def _():
+                hop(way, j).wait_recv()
+                if j + 1 < lines - 1:
+                    pl.when(has(way, -1))(hop(way, j + 1).start)
+                for e in range(1, n_groups):
+                    hop_over(way, j, e).start()
 
     op = wide // n_groups
     mine = pl.ds(pl.multiple_of(grp * op, op), op)
@@ -211,12 +228,40 @@
     y_peer = at(z * QUAD + lax.rem(q + half, QUAD))
     woy_sends = [remote(w_out.at[mine], wl.at[1, z, mine], s_woy.at[0], r_woy.at[0], y_peer)]
 
+    loads[1].wait()
+    expand(upw, ups)
     loads[2].wait()
     expand(dnw, dns)
 
-    loads[0].wait()
-    for c in winx_sends:
-        c.wait_recv()
+    for j in range(lines - 1):
+        for way in (1, -1):
+            @pl.when(has(way, j + 1))
+            def _():
+                for e in range(1, n_groups):
+                    hop_over(way, j, e).wait_recv()
+
+    qs = QUAD * cap
+    row = lax.broadcasted_iota(jnp.int32, (lanes, qs), 0)
+    col = lax.broadcasted_iota(jnp.int32, (lanes, qs), 1)
+
+    def spread(part):
+        expert = row - part * n - z * QUAD
+        inside = (expert >= 0) & (expert < QUAD) & (col >= expert * cap) & (col < expert * cap + cap)
+        return inside.astype(F32)
+
+    first = spread(0)
+    start = jnp.sum(first * ((row - z * QUAD) * cap).astype(F32), axis=0, keepdims=True)
+    first, second, third = first.astype(BF16), spread(1).astype(BF16), spread(2).astype(BF16)
+    slot = lax.broadcasted_iota(jnp.int32, (toks, qs), 1).astype(F32)
+    for s in range(lines):
+        if s > 0:
+            plan_sends[s - 1].wait_recv()
+        rank_x = jnp.dot(plan[s], first, preferred_element_type=F32)
+        hit = (rank_x + start == slot).astype(F32)
+        hits[s] = hit.astype(BF16)
+        ghi[s] = (hit * jnp.dot(plan[s], second, preferred_element_type=F32)).astype(BF16)
+        glo[s] = (hit * jnp.dot(plan[s], third, preferred_element_type=F32)).astype(BF16)
+
     for c in tok_sends:
         c.wait_recv()
 
@@ -236,78 +281,115 @@
     for d in range(1, QUAD):
         par_sends[d - 1].wait_recv()
         total = total + pr[d - 1].astype(F32)
-    lat[...] = total.astype(BF16)
-
-    disp[...] = lax.dot_general(
-        hits[...], lat[...], (((0,), (0,)), ((), ())), preferred_element_type=F32
-    ).astype(BF16)
+    lat[0] = total.astype(BF16)
+
+    def lat_send(s):
+        return along(s, lat.at[0], lat.at[s], s_lat.at[s], r_lat.at[s])
+
+    for s in range(1, lines):
+        lat_send(s).start()
 
     def block(i):
         return pl.ds(pl.multiple_of(i * cap, cap), cap)
 
-    def dispatch(d):
-        to = lax.rem(me + d, n)
-        return remote(disp.at[block(to)], rows_in.at[block(d)], s_disp.at[d], r_disp.at[d], at(to))
-
-    def give_back(d):
-        to = lax.rem(me + n - d, n)
-        return remote(res.at[block(d)], back.at[block(me)], s_ret.at[d], r_ret.at[d], at(to))
-
-    for d in range(1, n):
-        dispatch(d).start()
-    rows_in[0:cap] = disp[block(me)]
-
-    woy_sends[0].start()
+    def dispatch(s, d):
+        to, i = lax.rem(q + d, QUAD), s * QUAD + d
+        return remote(
+            disp.at[block(s * QUAD + to)], rows_in.at[block(i)], s_disp.at[i], r_disp.at[i], at(z * QUAD + to)
+        )
+
+    def give_back(s, d):
+        to, i = lax.rem(q + QUAD - d, QUAD), s * QUAD + d
+        return remote(
+            res.at[block(i)], back.at[block(s * QUAD + q)], s_ret.at[i], r_ret.at[i], at(z * QUAD + to)
+        )
+
+    def share_send(s):
+        to = lax.rem(z + lines - s, lines) * QUAD + q
+        return remote(mine_part.at[s], parts.at[s], s_sum.at[s], r_sum.at[s], at(to))
+
+    def rows_of(s):
+        return pl.ds(pl.multiple_of(s * qs, qs), qs)
+
+    def send_rows(s):
+        disp[rows_of(s)] = lax.dot_general(
+            hits[s], lat[s], (((0,), (0,)), ((), ())), preferred_element_type=F32
+        ).astype(BF16)
+        for d in range(1, QUAD):
+            dispatch(s, d).start()
+        rows_in[block(s * QUAD)] = disp[block(s * QUAD + q)]
+
+    def collect(s):
+        for d in range(1, QUAD):
+            give_back(s, d).wait_recv()
+        rows = back[rows_of(s)]
+        mine_part[s] = (
+            jnp.dot(ghi[s], rows, preferred_element_type=F32)
+            + jnp.dot(glo[s], rows, preferred_element_type=F32)
+        ).astype(BF16)
+        pl.when(s > 0)(lambda: share_send(s).start())
+
     wox_sends = []
 
     def over_groups(ref):
+        made = []
         for e in range(1, n_groups):
             i = len(wox_sends)
             c = remote(ref, ref, s_wox.at[i], r_wox.at[i], across(e))
-            c.start()
             wox_sends.append(c)
-
+            made.append(c)
+        return made
+
+    near, far = [], []
     for d in range(1, lines):
-        wo_sends[d - 1].wait_recv()
         frm = lax.rem(z + lines - d, lines)
-        c = remote(wl.at[0, frm, mine], wl.at[1, frm, mine], s_woy.at[d], r_woy.at[d], y_peer)
-        c.start()
-        woy_sends.append(c)
-        over_groups(wl.at[0, frm, mine])
-
-    def chunk(k, carry):
-        for i in range(CHUNK):
-            d = k * CHUNK + i
-
-            @pl.when(d > 0)
-            def _():
-                dispatch(d).wait_recv()
-
-        rows = pl.ds(pl.multiple_of(k * CHUNK * cap, CHUNK * cap), CHUNK * cap)
+        woy_sends.append(
+            remote(wl.at[0, frm, mine], wl.at[1, frm, mine], s_woy.at[d], r_woy.at[d], y_peer)
+        )
+        near += over_groups(wl.at[0, frm, mine])
+    for d in range(lines):
+        far += over_groups(wl.at[1, lax.rem(z + lines - d, lines), mine])
+
+    send_rows(0)
+
+    def chunk(s, carry):
+        @pl.when(s + 1 < lines)
+        def _():
+            lat_send(s + 1).wait_recv()
+            send_rows(s + 1)
+
+        for d in range(1, QUAD):
+            dispatch(s, d).wait_recv()
+
+        @pl.when(s == 1)
+        def _():
+            woy_sends[0].start()
+            for c in wo_sends:
+                c.wait_recv()
+            for c in woy_sends[1:] + near:
+                c.start()
+
+        rows = rows_of(s)
         hidden = jnp.dot(rows_in[rows], upw[...], preferred_element_type=F32)
         act[...] = jnp.square(jnp.maximum(hidden, 0.0)).astype(BF16)
         res[rows] = jnp.dot(act[...], dnw[...], preferred_element_type=F32).astype(BF16)
-        for i in range(CHUNK):
-            d = k * CHUNK + i
-
-            @pl.when(d > 0)
-            def _():
-                give_back(d).start()
-
+        for d in range(1, QUAD):
+            give_back(s, d).start()
+        back[block(s * QUAD + q)] = res[block(s * QUAD)]
+        pl.when(s > 0)(lambda: collect(s - 1))
         return carry
 
-    lax.fori_loop(0, n // CHUNK, chunk, 0)
-
-    for d in range(lines):
-        woy_sends[d].wait_recv()
-        over_groups(wl.at[1, lax.rem(z + lines - d, lines), mine])
-
-    back[block(me)] = res[0:cap]
-    for d in range(1, n):
-        give_back(d).wait_recv()
-    combined = jnp.dot(ghi[...], back[...], preferred_element_type=F32) + jnp.dot(
-        glo[...], back[...], preferred_element_type=F32
-    )
+    lax.fori_loop(0, lines, chunk, 0)
+    collect(lines - 1)
+
+    for c in woy_sends:
+        c.wait_recv()
+    for c in far:
+        c.start()
+    combined = mine_part[0].astype(F32)
+    for s in range(1, lines):
+        share_send(s).wait_recv()
+        combined = combined + parts[s].astype(F32)
     comb[0:toks] = combined.astype(BF16)
     pair = at(z * QUAD + q + 1 - 2 * lax.rem(q, 2))
     share = remote(comb.at[0:toks], comb.at[toks : 2 * toks], s_comb, r_comb, pair)
@@ -338,11 +420,26 @@
         hand_over(i).wait_recv()
     final = pltpu.make_async_copy(out_v, out, s_local.at[4])
     final.start()
-    for c in win_sends + winx_sends + tok_sends + par_sends + wo_sends + woy_sends + wox_sends + [share]:
+    for c in plan_sends + tok_sends + par_sends + wo_sends + woy_sends + wox_sends + [share]:
         c.wait_send()
-    for d in range(1, n):
-        dispatch(d).wait_send()
-        give_back(d).wait_send()
+    for j in range(lines - 1):
+        for way in (1, -1):
+            @pl.when(has(way, j) & has(way, -1))
+            def _():
+                hop(way, j).wait_send()
+
+            @pl.when(has(way, j + 1))
+            def _():
+                for e in range(1, n_groups):
+                    hop_over(way, j, e).wait_send()
+
+    for s in range(lines):
+        for d in range(1, QUAD):
+            dispatch(s, d).wait_send()
+            give_back(s, d).wait_send()
+        if s > 0:
+            lat_send(s).wait_send()
+            share_send(s).wait_send()
     for i in range(2 * lines):
         hand_over(i).wait_send()
     final.wait()
@@ -382,25 +479,28 @@
             vm(QUAD - 1, toks, lines * kd),
             vm(QUAD - 1, toks, wide),
             vm(QUAD - 1, toks, wide),
-            vm(toks, wide),
-            vm(toks, slots),
-            vm(toks, slots),
-            vm(toks, slots),
+            vm(lines, toks, -(-3 * n // 128) * 128),
+            vm(lines, toks, wide),
+            vm(lines, toks, QUAD * cap),
+            vm(lines, toks, QUAD * cap),
+            vm(lines, toks, QUAD * cap),
             vm(slots, wide),
             vm(slots, wide),
             vm(slots, wide),
             vm(slots, wide),
+            vm(lines, toks, wide),
+            vm(lines, toks, wide),
             vm(wide, hid),
             vm(hid, wide),
-            vm(CHUNK * cap, hid),
+            vm(QUAD * cap, hid),
             vm(2, lines, wide, wd),
             vm(2 * toks, wide),
-            vm(16, 128),
             vm(2 * lines, toks, wd),
             vm(toks, wd * n),
             sem(5), sem(n),
-            sem(lines), sem(lines), sem(lines * others + 1), sem(lines * others + 1),
+            sem(2 * lines), sem(2 * lines), sem(2 * lines * n_groups), sem(2 * lines * n_groups),
             sem(QUAD), sem(QUAD), sem(QUAD), sem(QUAD),
+            sem(lines), sem(lines), sem(lines), sem(lines), sem(lines), sem(lines),
             sem(n), sem(n), sem(n), sem(n),
             sem(lines), sem(lines), sem(lines), sem(lines),
             sem(2 * lines * others + 1), sem(2 * lines * others + 1),
@@ -426,7 +526,6 @@
         tokens, weight_in, weight_out, up_quant = args[:4]
         fits = (
             n % QUAD == 0
-            and (n // CHUNK) * CHUNK == n
             and up_quant.shape[0] == 1
             and weight_in.shape[0] % 128 == 0
             and weight_out.shape[1] % 128 == 0

time: 151 us -> 159 us (1.053)
  the two profiles are of different devices: /device:TPU:0 before, /device:TPU:17 now
where the time goes in v2:
time: 159 us; the launch traced here: 158 us
  Pallas kernels  151 us (95%)
  local copies, waits for them, and re-layouts  7.4 us (5%)
    pallas_call x1, Pallas kernels, kernel_body(): pl.pallas_call(functools.partial(layer_kernel, n, n_groups, cap), out_sha...  151 us
    unnamed x10, local copies, waits for them, and re-layouts  7.4 us

profile of v2, /device:TPU:17, one launch (start us, length us, event | category | flops | bytes accessed | tf_op | source)
XLA Modules:
  0.0 158.2 jit_solution(903731740606786592)
XLA Ops:
  0.0 0.8 copy.10
  0.8 0.8 copy.11.routing
  1.6 0.8 copy.12.gates
  2.3 0.0 copy-start
  2.4 1.0 copy-done
  3.4 0.0 copy-start.1
  3.4 1.0 copy-done.1
  4.4 0.0 copy-start.2
  4.4 0.7 copy-done.2
  5.1 150.8 %shard_map.91 = bf16[128,4096]{1,0:T(8,128)(2,1)} custom-call(bf16[128,4096]{1,0:T(8,128)(2,1)} %tokens.1, bf16[256,1024]{1,0:T(8,128)(2,1)S(1)} %copy-done, bf16[1024,256]{1,0:T(8,128)(2,1)S(1)} %copy-done.1, bf16[1024,2688]{1,0:T(8,128)(2,1)} %bitcast.6, f32[8,21]{1,0:T(8,128)S(1)} %bitcast.5, bf16[2688,1024]{1,0:T(8,128)(2,1)} %bitcast.7, ...), custom_call_target="tpu_custom_call" | custom-call | flops 10603200512 | bytes 33554432 | tf_op jit(solution)/shard_map/pallas_call | solution.py:471
  155.9 2.3 %copy.14 = bf16[128,4096]{1,0:T(8,128)(2,1)} copy(bf16[128,4096]{1,0:T(8,128)(2,1)} %shard_map.91) | data formatting | bytes 2097152
Async XLA Ops:
  2.3 1.0 copy-start
  3.4 1.0 copy-start.1
  4.4 0.7 copy-start.2

commit v3 on v2

--- a/solution.py
+++ b/solution.py
@@ -227,6 +227,7 @@
         wo_sends.append(c)
     y_peer = at(z * QUAD + lax.rem(q + half, QUAD))
     woy_sends = [remote(w_out.at[mine], wl.at[1, z, mine], s_woy.at[0], r_woy.at[0], y_peer)]
+    woy_sends[0].start()
 
     loads[1].wait()
     expand(upw, ups)
@@ -346,11 +347,15 @@
         woy_sends.append(
             remote(wl.at[0, frm, mine], wl.at[1, frm, mine], s_woy.at[d], r_woy.at[d], y_peer)
         )
-        near += over_groups(wl.at[0, frm, mine])
+        near.append(over_groups(wl.at[0, frm, mine]))
     for d in range(lines):
-        far += over_groups(wl.at[1, lax.rem(z + lines - d, lines), mine])
+        far.append(over_groups(wl.at[1, lax.rem(z + lines - d, lines), mine]))
 
     send_rows(0)
+    for d in range(1, lines):
+        wo_sends[d - 1].wait_recv()
+        for c in [woy_sends[d]] + near[d - 1]:
+            c.start()
 
     def chunk(s, carry):
         @pl.when(s + 1 < lines)
@@ -361,13 +366,12 @@
         for d in range(1, QUAD):
             dispatch(s, d).wait_recv()
 
-        @pl.when(s == 1)
+        @pl.when(s == max(lines - 2, 0))
         def _():
-            woy_sends[0].start()
-            for c in wo_sends:
-                c.wait_recv()
-            for c in woy_sends[1:] + near:
-                c.start()
+            for d in range(lines):
+                woy_sends[d].wait_recv()
+                for c in far[d]:
+                    c.start()
 
         rows = rows_of(s)
         hidden = jnp.dot(rows_in[rows], upw[...], preferred_element_type=F32)
@@ -382,10 +386,6 @@
     lax.fori_loop(0, lines, chunk, 0)
     collect(lines - 1)
 
-    for c in woy_sends:
-        c.wait_recv()
-    for c in far:
-        c.start()
     combined = mine_part[0].astype(F32)
     for s in range(1, lines):
         share_send(s).wait_recv()

time: 159 us -> 130 us (0.82)
  the two profiles are of different devices: /device:TPU:17 before, /device:TPU:0 now
where the time goes in v3:
time: 130 us; the launch traced here: 128 us
  Pallas kernels  121 us (93%)
  local copies, waits for them, and re-layouts  7.4 us (6%)
    pallas_call x1, Pallas kernels, kernel_body(): pl.pallas_call(functools.partial(layer_kernel, n, n_groups, cap), out_sha...  121 us
    unnamed x10, local copies, waits for them, and re-layouts  7.4 us

profile of v3, /device:TPU:0, one launch (start us, length us, event | category | flops | bytes accessed | tf_op | source)
XLA Modules:
  0.0 128.0 jit_solution(5444452030611154124)
XLA Ops:
  0.0 0.8 copy.10
  0.8 0.8 copy.11.routing
  1.6 0.8 copy.12.gates
  2.3 0.0 copy-start
  2.4 1.0 copy-done
  3.4 0.0 copy-start.1
  3.4 1.0 copy-done.1
  4.4 0.0 copy-start.2
  4.4 0.7 copy-done.2
  5.1 120.6 %shard_map.91 = bf16[128,4096]{1,0:T(8,128)(2,1)} custom-call(bf16[128,4096]{1,0:T(8,128)(2,1)} %tokens.1, bf16[256,1024]{1,0:T(8,128)(2,1)S(1)} %copy-done, bf16[1024,256]{1,0:T(8,128)(2,1)S(1)} %copy-done.1, bf16[1024,2688]{1,0:T(8,128)(2,1)} %bitcast.6, f32[8,21]{1,0:T(8,128)S(1)} %bitcast.5, bf16[2688,1024]{1,0:T(8,128)(2,1)} %bitcast.7, ...), custom_call_target="tpu_custom_call" | custom-call | flops 10603200512 | bytes 33554432 | tf_op jit(solution)/shard_map/pallas_call | solution.py:471
  125.7 2.3 %copy.14 = bf16[128,4096]{1,0:T(8,128)(2,1)} copy(bf16[128,4096]{1,0:T(8,128)(2,1)} %shard_map.91) | data formatting | bytes 2097152
Async XLA Ops:
  2.3 1.0 copy-start
  3.4 1.0 copy-start.1
  4.4 0.7 copy-start.2
